TPU v7x, 128 devices: a whole 4x4x4 slice. The times are simulated.
128 devices in a mesh: group: 8 (over y, core), sub: 16 (over z, x).
Axes of the slice: x: 4, y: 4, z: 4, core: 2. Of those that a mesh axis runs over, the one named last changes fastest.
Arguments:
- observations: float32 [64, 262144], P(None, ('group', 'sub')), may hold values from -6 to 6
- order: int32 [262144], P(('group', 'sub')), may hold values from 0 to 32767, as said below
- leaf_blocks: float32 [256, 1024, 1024], P(('group', 'sub')), as said below
- factors: float32 [8, 32, 262144], P(None, None, ('group', 'sub'))
Outputs:
- solution: float32 [64, 262144], P(None, ('group', 'sub'))
- residual: float32 [64, 262144], P(None, ('group', 'sub'))
Inputs may be any that keep to these rules, and one draw needn't show every extreme that they name: `order`: within each aligned block of 32768 entries, every value 0 .. 32767 appears once. `leaf_blocks`: every block is symmetric positive definite.
All inputs are finite; a program needn't handle non-finite values.
Results may differ from a plain program's by a relative error of at most 0.0003.
Values sent between devices are 32-bit elements; how exact they have to be, the bound alone decides.
A program may use at most 128 MiB of HBM per device.

v0:
```python
import jax
import jax.numpy as jnp
from jax import lax
from jax.sharding import PartitionSpec as P

ITERS = 4


def swapped(shard, axis, stride):
    return lax.ppermute(shard, axis, [(i, i ^ 1 << stride) for i in range(lax.axis_size(axis))])


def inner(left, right):
    return jnp.dot(left, right.T, precision=lax.Precision.HIGHEST)


def solve_spd(matrix, target):
    lower = jnp.linalg.cholesky(matrix)
    return jax.scipy.linalg.cho_solve((lower, True), target)


def node_sums(device_part):
    sub_bits = lax.axis_size("sub").bit_length() - 1
    group_bits = lax.axis_size("group").bit_length() - 1
    summed = device_part
    for bit in range(sub_bits):
        summed = summed.at[bit:].add(swapped(summed[bit:], "sub", bit))
    for bit in range(group_bits):
        first = sub_bits + bit
        summed = summed.at[first:].add(swapped(summed[first:], "group", bit))
    return summed


def apply_matrix(field, leaf_blocks, factors):
    rhs, rows = field.shape
    leaves_dev, leaf = (leaf_blocks.shape[0], leaf_blocks.shape[1])
    levels, rank = (factors.shape[0], factors.shape[1])
    local_bits = leaves_dev.bit_length() - 1
    split = field.reshape(rhs, leaves_dev, leaf)
    result = jnp.einsum("rbj,bjk->rbk", split, leaf_blocks, precision=lax.Precision.HIGHEST)
    basis = factors.reshape(levels, rank, leaves_dev, leaf)
    leaf_part = jnp.einsum("rbj,lkbj->lbrk", split, basis, precision=lax.Precision.HIGHEST)
    width = 2**1
    grouped = leaf_part[0].reshape(leaves_dev // width, width, rhs, rank)
    summed = jnp.sum(grouped, 1, keepdims=True)
    coefs = [jnp.broadcast_to(summed, grouped.shape).reshape(leaves_dev, rhs, rank)]
    device_part = jnp.sum(leaf_part[local_bits:], 1).reshape(levels - local_bits, rhs * rank)
    summed_nodes = node_sums(device_part).reshape(levels - local_bits, 1, rhs, rank)
    upper = jnp.broadcast_to(summed_nodes, (levels - local_bits, leaves_dev, rhs, rank))
    every = jnp.concatenate([jnp.stack(coefs, 0), upper], 0)
    result = result + jnp.einsum("lbrk,lkbj->rbj", every, basis, precision=lax.Precision.HIGHEST)
    return result.reshape(rhs, rows)


def shards(observations, order, leaf_blocks, factors):
    piece = lax.all_gather(observations, "sub", axis=1, tiled=True)
    count = piece.shape[1]
    valid = (order >= 0) & (order < count)
    values = jnp.take(piece, jnp.clip(order, 0, count - 1), axis=1)
    right = jnp.where(valid[None, :], values, 0.0)
    solution = jnp.zeros_like(right)
    residual = right
    direction = right
    norm_now = lax.psum(inner(residual, residual), ("group", "sub"))
    for step in range(ITERS):
        image = apply_matrix(direction, leaf_blocks, factors)
        curv = lax.psum(inner(direction, image), ("group", "sub"))
        alpha = solve_spd(curv, norm_now)
        solution = solution + jnp.dot(alpha.T, direction, precision=lax.Precision.HIGHEST)
        residual = residual - jnp.dot(alpha.T, image, precision=lax.Precision.HIGHEST)
        if step + 1 < ITERS:
            fresh = lax.psum(inner(residual, residual), ("group", "sub"))
        if step + 1 < ITERS:
            beta = solve_spd(norm_now, fresh)
            direction = residual + jnp.dot(beta.T, direction, precision=lax.Precision.HIGHEST)
            norm_now = fresh
    return (solution, residual)


def solution(mesh):
    in_specs = (
        P(None, ("group", "sub")),
        P(("group", "sub")),
        P(("group", "sub"), None, None),
        P(None, None, ("group", "sub")),
    )
    out_specs = (P(None, ("group", "sub")), P(None, ("group", "sub")))
    return jax.shard_map(shards, mesh=mesh, in_specs=in_specs, out_specs=out_specs, check_vma=False)
```

profile of v0, /device:TPU:1, one launch (start us, length us, event | category | flops | bytes accessed | tf_op | source)
XLA Modules:
  0.0 899.6 jit_solution(12372636154221389659)
XLA Ops:
  11.4 113.4 %all-gather.2.cloned.1.call-done = f32[64,32768]{0,1:T(8,128)} async-done(((f32[64,2048]{0,1:T(8,128)}), f32[64,32768]{0,1:T(8,128)}) %all-gather.2.cloned.1.call-update) | async-done | bytes 8388624 | tf_op jit(solution)/shard_map/all_gather | solution.py:56
  124.8 13.3 %gather_fusion = f32[2048,64]{1,0:T(8,128)} fusion(f32[64,32768]{0,1:T(8,128)} %all-gather.2.cloned.1.call-done, s32[2048]{0:T(1024)S(1)} %fusion.109), kind=kCustom, calls=%fused_computation | custom fusion | bytes 1056768 | tf_op jit(solution)/shard_map/jit(_take)/gather | solution.py:59
  159.0 5.4 collective-permute-start.4
  174.0 7.5 fusion
  182.3 67.1 %all-reduce = (f32[64,64]{0,1:T(8,128)S(1)}, f32[64,64]{0,1:T(8,128)S(1)}) all-reduce(f32[64,64]{0,1:T(8,128)S(1)} %fusion.27, f32[64,64]{0,1:T(8,128)S(1)} %fusion.29), channel_id=1, replica_groups=mesh['group'=8,'sub'=16] {'group','sub'}, use_global_device_ids=true, to_apply=%region_5.7 | all-reduce | flops 8192 | bytes 65536 | tf_op jit(solution)/shard_map/psum | solution.py:64
  249.5 5.8 cholesky.119
  264.3 62.7 %psum.58 = f32[64,64]{0,1:T(8,128)S(1)} all-reduce(f32[64,64]{0,1:T(8,128)S(1)} %fusion.126), channel_id=1, replica_groups=mesh['group'=8,'sub'=16] {'group','sub'}, use_global_device_ids=true, to_apply=%region_6.9 | all-reduce | flops 4096 | bytes 32768 | tf_op jit(solution)/shard_map/psum | solution.py:72
  327.1 5.8 cholesky.130
  361.8 7.2 cholesky.152
  388.6 5.7 custom-call.16
  397.2 7.5 fusion.1
  406.1 63.5 %psum.59 = f32[64,64]{0,1:T(8,128)S(1)} all-reduce(f32[64,64]{0,1:T(8,128)S(1)} %fusion.127), channel_id=1, replica_groups=mesh['group'=8,'sub'=16] {'group','sub'}, use_global_device_ids=true, to_apply=%region_9.12 | all-reduce | flops 4096 | bytes 32768 | tf_op jit(solution)/shard_map/psum | solution.py:67
  469.8 5.8 cholesky.141
  485.6 63.2 %psum.60 = f32[64,64]{0,1:T(8,128)S(1)} all-reduce(f32[64,64]{0,1:T(8,128)S(1)} %fusion.128), channel_id=1, replica_groups=mesh['group'=8,'sub'=16] {'group','sub'}, use_global_device_ids=true, to_apply=%region_10.13 | all-reduce | flops 4096 | bytes 32768 | tf_op jit(solution)/shard_map/psum | solution.py:72
  572.1 7.2 cholesky.174
  598.2 5.7 custom-call.18
  607.1 7.5 fusion.2
  616.0 64.1 %psum.61 = f32[64,64]{0,1:T(8,128)S(1)} all-reduce(f32[64,64]{0,1:T(8,128)S(1)} %fusion.129), channel_id=1, replica_groups=mesh['group'=8,'sub'=16] {'group','sub'}, use_global_device_ids=true, to_apply=%region_13.16 | all-reduce | flops 4096 | bytes 32768 | tf_op jit(solution)/shard_map/psum | solution.py:67
  680.2 5.8 cholesky.163
  696.6 63.0 %psum.62 = f32[64,64]{1,0:T(8,128)S(1)} all-reduce(f32[64,64]{1,0:T(8,128)S(1)} %fusion.130), channel_id=1, replica_groups=mesh['group'=8,'sub'=16] {'group','sub'}, use_global_device_ids=true, to_apply=%region_14.17 | all-reduce | flops 4096 | bytes 32768 | tf_op jit(solution)/shard_map/psum | solution.py:72
  784.8 5.2 collective-permute-start.25
  805.4 7.5 fusion.3
  813.6 63.2 %psum.63 = f32[64,64]{0,1:T(8,128)S(1)} all-reduce(f32[64,64]{0,1:T(8,128)S(1)} %fusion.131), channel_id=1, replica_groups=mesh['group'=8,'sub'=16] {'group','sub'}, use_global_device_ids=true, to_apply=%region_17.20 | all-reduce | flops 4096 | bytes 32768 | tf_op jit(solution)/shard_map/psum | solution.py:67
  876.9 5.8 cholesky.185
  (315 shorter events, 214.5 us)
Async XLA Ops:
  7.2 117.7 %all-gather.2.cloned.1.call-start = ((), (), s32[]{:S(2)}) async-start(), calls=%async_computation | async-start | bytes 17825792 | tf_op jit(solution)/shard_map/all_gather | solution.py:56
  143.4 3.2 collective-permute-start
  146.6 4.7 collective-permute-start.1
  151.4 3.2 collective-permute-start.2
  154.6 4.3 collective-permute-start.3
  159.0 6.3 collective-permute-start.4
  168.0 4.1 collective-permute-start.6
  352.8 4.9 collective-permute-start.8
  359.2 9.8 %collective-permute-start.9 = (f32[5,2048]{1,0:T(8,128)}, f32[5,2048]{1,0:T(8,128)}, u32[]{:S(2)}, u32[]{:S(2)}) collective-permute-start(f32[5,2048]{1,0:T(8,128)} %slice.657), channel_id=1, source_target_pairs={{0,4},{1,5},{2,6},{3,7},{4,0},{5,1},{6,2},{7,3},{8,12},{9,13},{10,... | collective-permute-start | bytes 122888 | tf_op jit(solution)/shard_map/ppermute | solution.py:10
  369.9 4.3 collective-permute-start.10
  374.9 7.7 collective-permute-start.11
  386.1 8.4 collective-permute-start.13
  558.6 3.2 collective-permute-start.14
  563.3 4.9 collective-permute-start.15
  569.7 9.7 %collective-permute-start.16 = (f32[5,2048]{1,0:T(8,128)}, f32[5,2048]{1,0:T(8,128)}, u32[]{:S(2)}, u32[]{:S(2)}) collective-permute-start(f32[5,2048]{1,0:T(8,128)} %slice.665), channel_id=1, source_target_pairs={{0,4},{1,5},{2,6},{3,7},{4,0},{5,1},{6,2},{7,3},{8,12},{9,13},{10,... | collective-permute-start | bytes 122888 | tf_op jit(solution)/shard_map/ppermute | solution.py:10
  580.2 4.3 collective-permute-start.17
  585.2 7.8 collective-permute-start.18
  596.5 7.6 collective-permute-start.20
  771.2 4.7 collective-permute-start.22
  775.9 3.2 collective-permute-start.23
  779.2 4.3 collective-permute-start.24
  784.8 9.8 %collective-permute-start.25 = (f32[3,2048]{1,0:T(4,128)}, f32[3,2048]{1,0:T(4,128)}, u32[]{:S(2)}, u32[]{:S(2)}) collective-permute-start(f32[3,2048]{1,0:T(4,128)} %slice.675), channel_id=1, source_target_pairs={{0,16},{16,0},{32,48},{48,32},{64,80},{80,64},{96,112},{112,96},{1... | collective-permute-start | bytes 73736 | tf_op jit(solution)/shard_map/ppermute | solution.py:10
  795.4 3.7 collective-permute-start.26
  799.1 4.1 collective-permute-start.27
  (37 other events, 684.4 us)
Sparse Core Ops, SparseCore 0:
  10.1 114.6 all-gather.1
where the time goes:
time: 910 us; the launch traced here: 900 us
  blocking collectives  447 us (49%)
  waiting for transfers between devices  147 us (16%)
  other arithmetic  106 us (12%)
  matrix products  76.3 us (8%)
  starting transfers between devices  55.5 us (6%)
  local copies, waits for them, and re-layouts  52.2 us (6%)
  between operations  15.9 us (2%)
    psum x3, blocking collectives, shards(): curv = lax.psum(inner(direction, image), ('group', 'sub'))  191 us
    psum x3, blocking collectives, shards(): fresh = lax.psum(inner(residual, residual), ('group', 'sub'))  189 us
    all_gather x1, waiting for transfers between devices, shards(): piece = lax.all_gather(observations, 'sub', axis=1, tiled=True)  113 us
    psum x1, blocking collectives, shards(): norm_now = lax.psum(inner(residual, residual), ('group', 'sub'))  67.1 us
    ppermute x28, starting transfers between devices, swapped(): lax.ppermute(shard, axis, [(i, i ^ 1 << stride) for i in range(lax.axis_s...  55.5 us
    another operation x21, other arithmetic, solve_spd(): lower = jnp.linalg.cholesky(matrix)  50.1 us
    another operation x14, other arithmetic, solve_spd(): return jax.scipy.linalg.cho_solve((lower, True), target)  43 us
    ppermute x28, waiting for transfers between devices, swapped(): lax.ppermute(shard, axis, [(i, i ^ 1 << stride) for i in range(lax.axis_s...  33.3 us
  transfers between devices with their start and end apart: 29, of which 20 were waited for; matrix products, arithmetic and copies ran while one was open for 6% of the time, Pallas kernels for 0%

commit v1 on v0

v1 whole, which is shorter than its diff:
```python
import functools

import jax
import jax.numpy as jnp
from jax import lax
from jax.experimental import pallas as pl
from jax.experimental.pallas import tpu as pltpu
from jax.sharding import PartitionSpec as P

ITERS = 4
MESH = pl.DeviceIdType.MESH
F32 = jnp.float32
BF16 = jnp.bfloat16
EXACT = lax.Precision.HIGHEST
NT = (((1,), (1,)), ((), ()))


def halves(x):
    high = x.astype(BF16)
    return high, (x - high.astype(F32)).astype(BF16)


def dot3(left, right_high, right_low, dims=(((1,), (0,)), ((), ()))):
    rows = left.shape[0]
    high, low = halves(left)
    both = lax.dot_general(
        jnp.concatenate([high, low], 0), right_high, dims, preferred_element_type=F32
    )
    rest = lax.dot_general(high, right_low, dims, preferred_element_type=F32)
    return both[:rows] + (both[rows:] + rest)


def dot_exact(left, right, dims=(((1,), (0,)), ((), ()))):
    return lax.dot_general(left, right, dims, precision=EXACT, preferred_element_type=F32)


def eliminate(systems):
    size = systems[0].shape[0]
    rows = lax.broadcasted_iota(jnp.int32, systems[0].shape, 0)
    for k in range(size):
        done = []
        for system in systems:
            scaled = system[k : k + 1, :] * (1.0 / system[k : k + 1, k : k + 1])
            done.append(jnp.where(rows == k, scaled, system - system[:, k : k + 1] * scaled))
        systems = done
    return systems


def coefficient_stage(pieces, low_tile, high_tile, low_lanes, high_lanes, leaf_lanes):
    tiles = len(pieces[0])
    pairs = [[pieces[2 * h][t] + pieces[2 * h + 1][t] for t in range(tiles)] for h in range(2)]
    total = [pairs[0][t] + pairs[1][t] for t in range(tiles)]
    lane = lax.broadcasted_iota(jnp.int32, pieces[0][0].shape, 1)
    in_low = (lane >= low_lanes) & (lane < low_lanes + 32)
    in_high = (lane >= high_lanes) & (lane < high_lanes + 32)
    parts = [
        jnp.where(in_low, pairs[0][low_tile], jnp.where(in_high, total[high_tile], 0.0)),
        jnp.where(in_low, pairs[1][low_tile], 0.0),
    ]
    if leaf_lanes:
        parts = parts + [jnp.zeros_like(parts[0])] * 2
        parts = [jnp.where(lane < 32, pieces[m][0], parts[m]) for m in range(4)]
    return pairs, total, parts


def node_products(parts):
    side = jnp.concatenate(parts, 1)
    return dot_exact(side, jnp.concatenate([jnp.zeros_like(side), side], 0), NT)


def kernel(
    obs_ref, order_ref, leaf_ref, factors_ref,
    solution_ref, residual_ref,
    stage, leaf_high, leaf_low, basis_high, basis_low, across_high, across_low,
    gathered, table, picked, order_in, order_smem, ready,
    r_ref, w_ref, d_ref, s_ref, x_ref, own_ref,
    x_coef, x_sum, z_coef, z_sum, c_coef, c_sum, y_coef, y_sum,
    load_sem, smem_sem, order_send, order_recv, obs_send, obs_recv, back_send, back_recv,
    ring_send, ring_recv,
):
    group, sub = lax.axis_index("group"), lax.axis_index("sub")
    x = lax.rem(sub, 4)
    z = lax.div(sub, 4)
    core = lax.rem(group, 2)
    y = lax.div(group, 2)
    rhs, points = obs_ref.shape
    width = rhs // 4

    loads = [
        pltpu.make_async_copy(leaf_ref.at[b], stage.at[b], load_sem.at[b]) for b in range(2)
    ]
    for load in loads:
        load.start()

    def on_x(k):
        return (group, z * 4 + (x ^ k))

    def on_z(k):
        return (group, (z ^ k) * 4 + x)

    def on_core(k):
        return (y * 2 + (core ^ k), sub)

    def on_y(k):
        return ((y ^ k) * 2 + core, sub)

    barrier = pltpu.get_barrier_semaphore()
    for k in range(1, 16):
        pl.semaphore_signal(barrier, inc=1, device_id=(group, sub ^ k), device_id_type=MESH)
    for k in range(1, 4):
        pl.semaphore_signal(barrier, inc=1, device_id=on_y(k), device_id_type=MESH)
    pl.semaphore_signal(barrier, inc=1, device_id=on_core(1), device_id_type=MESH)
    pl.semaphore_wait(barrier, 19)

    order_copies = []
    for k in range(1, 4):
        copy = pltpu.make_async_remote_copy(
            src_ref=order_ref, dst_ref=order_in.at[k],
            send_sem=order_send.at[k], recv_sem=order_recv.at[k],
            device_id=on_x(k), device_id_type=MESH,
        )
        copy.start()
        order_copies.append(copy)
    obs_copies = {}
    for k in (1, 4, 2, 3, 5, 7, 8, 12, 13, 6, 9, 10, 11, 14, 15):
        quarter = x ^ (k % 4)
        copy = pltpu.make_async_remote_copy(
            src_ref=obs_ref.at[pl.ds(pl.multiple_of(quarter * width, width), width), :],
            dst_ref=gathered.at[k],
            send_sem=obs_send.at[k], recv_sem=obs_recv.at[k],
            device_id=(group, sub ^ k), device_id_type=MESH,
        )
        copy.start()
        obs_copies[k] = copy

    for b in range(2):
        loads[b].wait()

        def cut(i, _, b=b):
            rows = pl.ds(pl.multiple_of(i * 64, 64), 64)
            leaf_high[b, rows, :], leaf_low[b, rows, :] = halves(stage[b, rows, :])
            return 0

        lax.fori_loop(0, leaf_ref.shape[1] // 64, cut, 0)

    def turn(i, _):
        cols = pl.ds(pl.multiple_of(i * 128, 128), 128)
        part = factors_ref[:, cols]
        basis_high[:, cols], basis_low[:, cols] = halves(part)
        across_high[cols, :], across_low[cols, :] = halves(part.T)
        return 0

    lax.fori_loop(0, points // 128, turn, 0)

    own_order = pltpu.make_async_copy(order_ref, order_smem.at[0], smem_sem.at[0])
    own_order.start()
    for k in range(1, 4):
        order_copies[k - 1].wait()
        copy = pltpu.make_async_copy(order_in.at[k], order_smem.at[k], smem_sem.at[k])
        copy.start()
        copy.wait()
    own_order.wait()

    def tabulate(block, k):
        def step(i, _):
            cols = pl.ds(pl.multiple_of(i * 128, 128), 128)
            rows = pl.ds(pl.multiple_of((sub ^ k) * points + i * 128, 128), 128)
            table[rows, :] = block(cols).T
            return 0

        lax.fori_loop(0, points // 128, step, 0)

    mine = pl.ds(pl.multiple_of(x * width, width), width)
    tabulate(lambda cols: obs_ref[mine, cols], 0)
    for k in (1, 4, 2, 3, 5, 7, 8, 12, 13, 6, 9, 10, 11, 14, 15):
        obs_copies[k].wait()
        tabulate(lambda cols, k=k: gathered[k, :, cols], k)

    back_copies = []
    for k in (2, 1, 3, 0):

        def pick(i, _, k=k):
            for j in range(128):
                picked[pl.ds(i * 128 + j, 1), :] = table[pl.ds(order_smem[k, i, j], 1), :]
            return 0

        lax.fori_loop(0, points // 128, pick, 0)

        def lay(i, _, k=k):
            cols = pl.ds(pl.multiple_of(i * 128, 128), 128)
            turned = picked[pl.ds(pl.multiple_of(i * 128, 128), 128), :].T
            if k:
                ready[k, :, cols] = turned
            else:
                r_ref[mine, cols] = turned
            return 0

        lax.fori_loop(0, points // 128, lay, 0)
        if k:
            copy = pltpu.make_async_remote_copy(
                src_ref=ready.at[k], dst_ref=r_ref.at[mine, :],
                send_sem=back_send.at[k], recv_sem=back_recv.at[k],
                device_id=on_x(k), device_id_type=MESH,
            )
            copy.start()
            back_copies.append(copy)
    for copy in back_copies:
        copy.wait()

    def send(kind, turn_at, buffer, slot, peer, count):
        copies = []
        for k in range(1, count):
            copy = pltpu.make_async_remote_copy(
                src_ref=buffer.at[turn_at, slot], dst_ref=buffer.at[turn_at, slot],
                send_sem=ring_send.at[kind, k], recv_sem=ring_recv.at[kind, turn_at, k],
                device_id=peer(k), device_id_type=MESH,
            )
            copy.start()
            copies.append(copy)
        return copies

    def finish(copies):
        for copy in copies:
            copy.wait()

    d_ref[...] = jnp.zeros_like(d_ref)
    s_ref[...] = jnp.zeros_like(s_ref)
    x_ref[...] = jnp.zeros_like(x_ref)
    half = points // 2
    lane = lax.broadcasted_iota(jnp.int32, (rhs, 128), 1)
    eye = (lax.broadcasted_iota(jnp.int32, (rhs, rhs), 0) == lax.broadcasted_iota(jnp.int32, (rhs, rhs), 1)).astype(F32)

    def iteration(step, carry):
        inverse, curv_before = carry
        at = lax.rem(step, 2)
        r = r_ref[...]
        own = dot3(r, across_high[...], across_low[...])
        x_coef[at, x] = own
        coef_copies = send(0, at, x_coef, x, on_x, 4)

        for b in range(2):
            cols = slice(b * half, (b + 1) * half)
            w_ref[:, cols] = dot3(r_ref[:, cols], leaf_high[b], leaf_low[b])
        rw_high, rw_low = halves(jnp.concatenate([r_ref[...], w_ref[...]], 0))
        x_sum[at, x] = dot3(r_ref[...], rw_high, rw_low, NT)
        sum_copies = send(1, at, x_sum, x, on_x, 4)

        finish(coef_copies)
        pieces = [[x_coef[at, m, :, 0:128], x_coef[at, m, :, 128:256]] for m in range(4)]
        pairs, total, parts = coefficient_stage(pieces, 0, 0, 32, 64, True)
        z_coef[at, z, :, 0:128] = total[0]
        z_coef[at, z, :, 128:256] = total[1]
        coef_copies = send(2, at, z_coef, z, on_z, 4)
        first = jnp.where(lane < 32, own[:, 0:128], jnp.where(x < 2, pairs[0][0], pairs[1][0]))
        first = jnp.where(lane < 64, first, total[0])
        extra = node_products(parts)
        finish(sum_copies)
        z_sum[at, z] = ((x_sum[at, 0] + x_sum[at, 1]) + (x_sum[at, 2] + x_sum[at, 3])) + extra
        sum_copies = send(3, at, z_sum, z, on_z, 4)

        finish(coef_copies)
        pieces = [[z_coef[at, m, :, 0:128], z_coef[at, m, :, 128:256]] for m in range(4)]
        pairs, total, parts = coefficient_stage(pieces, 0, 1, 96, 0, False)
        c_coef[at, core] = total[1]
        coef_copies = send(4, at, c_coef, core, on_core, 2)
        first = jnp.where(lane < 96, first, jnp.where(z < 2, pairs[0][0], pairs[1][0]))
        second = total[1]
        extra = node_products(parts)
        finish(sum_copies)
        c_sum[at, core] = ((z_sum[at, 0] + z_sum[at, 1]) + (z_sum[at, 2] + z_sum[at, 3])) + extra
        sum_copies = send(5, at, c_sum, core, on_core, 2)

        finish(coef_copies)
        chip = c_coef[at, 0] + c_coef[at, 1]
        y_coef[at, y] = chip
        coef_copies = send(6, at, y_coef, y, on_y, 4)
        second = jnp.where(lane < 32, second, chip)
        extra = node_products([jnp.where((lane >= 32) & (lane < 64), chip, 0.0)])
        finish(sum_copies)
        y_sum[at, y] = (c_sum[at, 0] + c_sum[at, 1]) + extra
        sum_copies = send(7, at, y_sum, y, on_y, 4)

        finish(coef_copies)
        pieces = [[y_coef[at, m]] for m in range(4)]
        pairs, total, parts = coefficient_stage(pieces, 0, 0, 64, 96, False)
        second = jnp.where(lane < 64, second, jnp.where(y < 2, pairs[0][0], pairs[1][0]))
        second = jnp.where(lane < 96, second, total[0])
        extra = node_products(parts)
        own_ref[:, 0:128] = first
        own_ref[:, 128:256] = second
        coefs = own_ref[...]
        for c in range(4):
            cols = slice(c * 512, (c + 1) * 512)
            w_ref[:, cols] = w_ref[:, cols] + dot3(coefs, basis_high[:, cols], basis_low[:, cols])
        finish(sum_copies)
        both = ((y_sum[at, 0] + y_sum[at, 1]) + (y_sum[at, 2] + y_sum[at, 3])) + extra

        norm, along = both[:, :rhs], both[:, rhs:]
        beta = dot_exact(inverse, norm)
        curv = along - dot_exact(beta.T, dot_exact(curv_before, beta))

        def weights(matrix):
            high, low = halves(matrix)
            high, low = high.astype(F32), low.astype(F32)
            return jnp.concatenate([high, high, low, low], 0).T.astype(BF16)

        def times(weight, array):
            high, low = halves(array)
            return jnp.dot(
                weight, jnp.concatenate([high, low, high, low], 0), preferred_element_type=F32
            )

        beta_weight = weights(beta)
        def advance(c, _):
            cols = pl.ds(pl.multiple_of(c * 512, 512), 512)
            d_ref[:, cols] = r_ref[:, cols] + times(beta_weight, d_ref[:, cols])
            s_ref[:, cols] = w_ref[:, cols] + times(beta_weight, s_ref[:, cols])
            return 0

        lax.fori_loop(0, 4, advance, 0)
        solved, inverted = eliminate(
            [jnp.concatenate([curv, norm], 1), jnp.concatenate([norm, eye], 1)]
        )
        alpha_weight = weights(solved[:, rhs:])

        def improve(c, _):
            cols = pl.ds(pl.multiple_of(c * 512, 512), 512)
            r_ref[:, cols] = r_ref[:, cols] - times(alpha_weight, s_ref[:, cols])
            x_ref[:, cols] = x_ref[:, cols] + times(alpha_weight, d_ref[:, cols])
            return 0

        lax.fori_loop(0, 4, improve, 0)
        return inverted[:, rhs:], curv

    zeros = jnp.zeros((rhs, rhs), F32)
    lax.fori_loop(0, ITERS, iteration, (zeros, zeros))
    solution_ref[...] = x_ref[...]
    residual_ref[...] = r_ref[...]


def shards(observations, order, leaf_blocks, factors):
    rhs, points = observations.shape
    leaves, leaf = leaf_blocks.shape[:2]
    rank = factors.shape[0] * factors.shape[1]
    width = rhs // 4
    vector = pltpu.VMEM((rhs, points), F32)
    dma = pltpu.SemaphoreType.DMA
    vmem = pl.BlockSpec(memory_space=pltpu.VMEM)
    out = jax.ShapeDtypeStruct((rhs, points), F32)
    return pl.pallas_call(
        kernel,
        out_shape=(out, out),
        in_specs=[vmem, vmem, pl.BlockSpec(memory_space=pl.ANY), vmem],
        out_specs=(vmem, vmem),
        scratch_shapes=[
            pltpu.VMEM((leaves, leaf, leaf), F32),
            pltpu.VMEM((leaves, leaf, leaf), BF16),
            pltpu.VMEM((leaves, leaf, leaf), BF16),
            pltpu.VMEM((rank, points), BF16),
            pltpu.VMEM((rank, points), BF16),
            pltpu.VMEM((points, rank), BF16),
            pltpu.VMEM((points, rank), BF16),
            pltpu.VMEM((16, width, points), F32),
            pltpu.VMEM((16 * points, width), F32),
            pltpu.VMEM((points, width), F32),
            pltpu.VMEM((4, points // 128, 128), jnp.int32),
            pltpu.SMEM((4, points // 128, 128), jnp.int32),
            pltpu.VMEM((4, width, points), F32),
            vector, vector, vector, vector, vector,
            pltpu.VMEM((rhs, rank), F32),
            pltpu.VMEM((2, 4, rhs, rank), F32),
            pltpu.VMEM((2, 4, rhs, 2 * rhs), F32),
            pltpu.VMEM((2, 4, rhs, rank), F32),
            pltpu.VMEM((2, 4, rhs, 2 * rhs), F32),
            pltpu.VMEM((2, 2, rhs, rank // 2), F32),
            pltpu.VMEM((2, 2, rhs, 2 * rhs), F32),
            pltpu.VMEM((2, 4, rhs, rank // 2), F32),
            pltpu.VMEM((2, 4, rhs, 2 * rhs), F32),
            dma((2,)), dma((4,)), dma((4,)), dma((4,)),
            dma((16,)), dma((16,)), dma((4,)), dma((4,)),
            dma((8, 4)), dma((8, 2, 4)),
        ],
        compiler_params=pltpu.CompilerParams(
            collective_id=0, has_side_effects=True, vmem_limit_bytes=60 * 2**20
        ),
        name="block_cg",
    )(observations, order.reshape(points // 128, 128), leaf_blocks, factors.reshape(rank, points))


def solution(mesh):
    in_specs = (
        P(None, ("group", "sub")),
        P(("group", "sub")),
        P(("group", "sub"), None, None),
        P(None, None, ("group", "sub")),
    )
    out_specs = (P(None, ("group", "sub")), P(None, ("group", "sub")))
    return jax.shard_map(shards, mesh=mesh, in_specs=in_specs, out_specs=out_specs, check_vma=False)
```

time: 910 us -> 180 us (0.20); the launches traced: 900 us -> 180 us
  blocking collectives: 447 us -> 0 us
  Pallas kernels: 0 us -> 175 us
  waiting for transfers between devices: 147 us -> 0 us
  other arithmetic: 106 us -> 0 us
  matrix products: 76.3 us -> 0 us
  starting transfers between devices: 55.5 us -> 0 us
  local copies, waits for them, and re-layouts: 52.2 us -> 3.74 us
  between operations: 15.9 us -> 0.64 us
    psum x7 -> x0, blocking collectives: 447 us -> none  [the longest x3 191 us: shards(): curv = lax.psum(inner(direction, image), ('group', 'sub'))]
    pallas_call x0 -> x1, Pallas kernels: none -> 175 us  [shards(): pl.pallas_call(kernel, out_shape=(out, out), in_specs=[vmem, vmem, pl.Blo...]
    all_gather x1 -> x0, waiting for transfers between devices: 113 us -> none  [shards(): piece = lax.all_gather(observations, 'sub', axis=1, tiled=True)]
    another operation x35 -> x0, other arithmetic: 93.1 us -> none  [the longest x21 50.1 us: solve_spd(): lower = jnp.linalg.cholesky(matrix)]
    dot_general x27 -> x0, matrix products: 59.8 us -> none  [the longest x4 30.2 us: apply_matrix(): jnp.einsum('rbj,bjk->rbk', split, leaf_blocks, precision=lax.Precision.HI...]
    ppermute x28 -> x0, starting transfers between devices: 55.5 us -> none  [swapped(): lax.ppermute(shard, axis, [(i, i ^ 1 << stride) for i in range(lax.axis_s...]
    ppermute x28 -> x0, waiting for transfers between devices: 33.3 us -> none  [swapped(): lax.ppermute(shard, axis, [(i, i ^ 1 << stride) for i in range(lax.axis_s...]
    gather x2 -> x0, local copies, waits for them, and re-layouts: 14.9 us -> none  [shards(): values = jnp.take(piece, jnp.clip(order, 0, count - 1), axis=1)]
  transfers between devices with their start and end apart: 29 -> 0, of which waited for: 20 -> 0; matrix products, arithmetic and copies ran while one was open for 6% -> 0% of each run, Pallas kernels for 0% -> 0%
where the time goes in v1:
time: 180 us
  Pallas kernels  175 us (97%)
  local copies, waits for them, and re-layouts  3.74 us (2%)
    pallas_call x1, Pallas kernels, shards(): pl.pallas_call(kernel, out_shape=(out, out), in_specs=[vmem, vmem, pl.Blo...  175 us
    unnamed x2, local copies, waits for them, and re-layouts  3.74 us

profile of v1, /device:TPU:1, one launch (start us, length us, event | category | flops | bytes accessed | tf_op | source)
XLA Modules:
  0.0 179.6 jit_solution(2651585418658455145)
XLA Ops:
  0.6 175.2 %block_cg.1 = (f32[64,2048]{1,0:T(8,128)}, f32[64,2048]{1,0:T(8,128)}) custom-call(f32[64,2048]{1,0:T(8,128)} %obs_ref.1, s32[16,128]{1,0:T(8,128)} %bitcast.3, f32[2,1024,1024]{2,1,0:T(8,128)} %leaf_ref.1, f32[256,2048]{1,0:T(8,128)} %bitcast.2), custom_call_target="tpu_custom_call" | custom-call | tf_op jit(solution)/shard_map/block_cg/pallas_call | solution.py:350
  175.8 1.9 %copy.8 = f32[64,2048]{1,0:T(8,128)} copy(f32[64,2048]{1,0:T(8,128)} %get-tuple-element.4) | data formatting | bytes 1048576
  177.7 1.9 %copy.9 = f32[64,2048]{1,0:T(8,128)} copy(f32[64,2048]{1,0:T(8,128)} %get-tuple-element.5) | data formatting | bytes 1048576

commit v2 on v1

--- a/solution.py
+++ b/solution.py
@@ -72,10 +72,10 @@
     obs_ref, order_ref, leaf_ref, factors_ref,
     solution_ref, residual_ref,
     stage, leaf_high, leaf_low, basis_high, basis_low, across_high, across_low,
-    gathered, table, picked, order_in, order_smem, ready,
+    gathered, table, picked, order_in, source_in, order_smem, ready,
     r_ref, w_ref, d_ref, s_ref, x_ref, own_ref,
     x_coef, x_sum, z_coef, z_sum, c_coef, c_sum, y_coef, y_sum,
-    load_sem, smem_sem, order_send, order_recv, obs_send, obs_recv, back_send, back_recv,
+    load_sem, smem_sem, order_send, order_recv, near_send, near_recv, far_send, far_recv, back_send, back_recv,
     ring_send, ring_recv,
 ):
     group, sub = lax.axis_index("group"), lax.axis_index("sub")
@@ -84,7 +84,6 @@
     core = lax.rem(group, 2)
     y = lax.div(group, 2)
     rhs, points = obs_ref.shape
-    width = rhs // 4
 
     loads = [
         pltpu.make_async_copy(leaf_ref.at[b], stage.at[b], load_sem.at[b]) for b in range(2)
@@ -104,44 +103,82 @@
     def on_y(k):
         return ((y ^ k) * 2 + core, sub)
 
+    def on_diagonal(j):
+        return (group, lax.rem(z + j, 4) * 4 + lax.rem(x + j, 4))
+
     barrier = pltpu.get_barrier_semaphore()
-    for k in range(1, 16):
-        pl.semaphore_signal(barrier, inc=1, device_id=(group, sub ^ k), device_id_type=MESH)
     for k in range(1, 4):
-        pl.semaphore_signal(barrier, inc=1, device_id=on_y(k), device_id_type=MESH)
+        for peer in (on_x(k), on_z(k), on_y(k), on_diagonal(k)):
+            pl.semaphore_signal(barrier, inc=1, device_id=peer, device_id_type=MESH)
     pl.semaphore_signal(barrier, inc=1, device_id=on_core(1), device_id_type=MESH)
-    pl.semaphore_wait(barrier, 19)
-
-    order_copies = []
-    for k in range(1, 4):
+    pl.semaphore_wait(barrier, 13)
+
+    def remote(source, target, sent, received, peer):
         copy = pltpu.make_async_remote_copy(
-            src_ref=order_ref, dst_ref=order_in.at[k],
-            send_sem=order_send.at[k], recv_sem=order_recv.at[k],
-            device_id=on_x(k), device_id_type=MESH,
+            src_ref=source, dst_ref=target, send_sem=sent, recv_sem=received,
+            device_id=peer, device_id_type=MESH,
         )
         copy.start()
-        order_copies.append(copy)
-    obs_copies = {}
-    for k in (1, 4, 2, 3, 5, 7, 8, 12, 13, 6, 9, 10, 11, 14, 15):
-        quarter = x ^ (k % 4)
-        copy = pltpu.make_async_remote_copy(
-            src_ref=obs_ref.at[pl.ds(pl.multiple_of(quarter * width, width), width), :],
-            dst_ref=gathered.at[k],
-            send_sem=obs_send.at[k], recv_sem=obs_recv.at[k],
-            device_id=(group, sub ^ k), device_id_type=MESH,
-        )
-        copy.start()
-        obs_copies[k] = copy
-
-    for b in range(2):
+        return copy
+
+    width = rhs // 8
+    by_x, by_z = slice(0, width), slice(width, 2 * width)
+
+    def x_rows(at):
+        return pl.ds(pl.multiple_of(at * width, width), width)
+
+    def z_rows(at):
+        return pl.ds(pl.multiple_of(rhs // 2 + at * width, width), width)
+
+    order_copies = [
+        remote(order_ref, order_in.at[4 - j], order_send.at[j], order_recv.at[4 - j], on_diagonal(j))
+        for j in range(1, 4)
+    ]
+    near = []
+    for k in range(1, 4):
+        near.append((
+            remote(obs_ref.at[x_rows(x ^ k), :], gathered.at[sub, by_x], near_send.at[0, k], near_recv.at[0, k], on_x(k)),
+            remote(obs_ref.at[z_rows(z ^ k), :], gathered.at[sub, by_z], near_send.at[1, k], near_recv.at[1, k], on_z(k)),
+        ))
+    far = []
+    for m in range(1, 4):
+        far.append(remote(obs_ref.at[x_rows(x), :], gathered.at[sub, by_x], far_send.at[0, 0, m], far_recv.at[0, 0, m], on_z(m)))
+        far.append(remote(obs_ref.at[z_rows(z), :], gathered.at[sub, by_z], far_send.at[1, 0, m], far_recv.at[1, 0, m], on_x(m)))
+    gathered[sub, by_x, :] = obs_ref[x_rows(x), :]
+    gathered[sub, by_z, :] = obs_ref[z_rows(z), :]
+
+    def cut_leaf(b):
         loads[b].wait()
 
-        def cut(i, _, b=b):
+        def cut(i, _):
             rows = pl.ds(pl.multiple_of(i * 64, 64), 64)
             leaf_high[b, rows, :], leaf_low[b, rows, :] = halves(stage[b, rows, :])
             return 0
 
         lax.fori_loop(0, leaf_ref.shape[1] // 64, cut, 0)
+
+    cut_leaf(0)
+    for k in range(1, 4):
+        from_x, from_z = near[k - 1]
+        from_x.wait()
+        slot = gathered.at[z * 4 + (x ^ k), by_x]
+        for m in range(1, 4):
+            far.append(remote(slot, slot, far_send.at[0, k, m], far_recv.at[0, k, m], on_z(m)))
+        from_z.wait()
+        slot = gathered.at[(z ^ k) * 4 + x, by_z]
+        for m in range(1, 4):
+            far.append(remote(slot, slot, far_send.at[1, k, m], far_recv.at[1, k, m], on_x(m)))
+
+    order_in[0] = order_ref[...]
+    for copy in order_copies:
+        copy.wait()
+    for j in range(4):
+        position = order_in[j]
+        source_in[j] = lax.rem(lax.div(position, points), 8)
+        order_in[j] = lax.div(position, points * 8) * points + lax.rem(position, points)
+    to_scalar = pltpu.make_async_copy(order_in, order_smem, smem_sem)
+    to_scalar.start()
+    cut_leaf(1)
 
     def turn(i, _):
         cols = pl.ds(pl.multiple_of(i * 128, 128), 128)
@@ -151,59 +188,50 @@
         return 0
 
     lax.fori_loop(0, points // 128, turn, 0)
-
-    own_order = pltpu.make_async_copy(order_ref, order_smem.at[0], smem_sem.at[0])
-    own_order.start()
-    for k in range(1, 4):
-        order_copies[k - 1].wait()
-        copy = pltpu.make_async_copy(order_in.at[k], order_smem.at[k], smem_sem.at[k])
-        copy.start()
+    to_scalar.wait()
+    for copy in far:
         copy.wait()
-    own_order.wait()
-
-    def tabulate(block, k):
-        def step(i, _):
-            cols = pl.ds(pl.multiple_of(i * 128, 128), 128)
-            rows = pl.ds(pl.multiple_of((sub ^ k) * points + i * 128, 128), 128)
-            table[rows, :] = block(cols).T
+
+    def tabulate(i, _):
+        for j in range(4):
+            cols = pl.ds(pl.multiple_of(i * 512 + j * 128, 128), 128)
+            for h in range(2):
+                rows = pl.ds(pl.multiple_of(h * points + i * 512 + j * 128, 128), 128)
+                table[rows, :] = gathered[8 * h : 8 * h + 8, :, cols].reshape(128, 128).T
+        return 0
+
+    lax.fori_loop(0, points // 512, tabulate, 0)
+
+    back_copies = []
+    for j in (2, 1, 3, 0):
+
+        def pick(i, _, j=j):
+            for n in range(128):
+                picked[pl.ds(i * 128 + n, 1), :] = table[pl.ds(order_smem[j, i, n], 1), :]
             return 0
 
-        lax.fori_loop(0, points // 128, step, 0)
-
-    mine = pl.ds(pl.multiple_of(x * width, width), width)
-    tabulate(lambda cols: obs_ref[mine, cols], 0)
-    for k in (1, 4, 2, 3, 5, 7, 8, 12, 13, 6, 9, 10, 11, 14, 15):
-        obs_copies[k].wait()
-        tabulate(lambda cols, k=k: gathered[k, :, cols], k)
-
-    back_copies = []
-    for k in (2, 1, 3, 0):
-
-        def pick(i, _, k=k):
-            for j in range(128):
-                picked[pl.ds(i * 128 + j, 1), :] = table[pl.ds(order_smem[k, i, j], 1), :]
+        lax.fori_loop(0, points // 128, pick, 0)
+
+        def lay(i, _, j=j):
+            for n in range(4):
+                cols = pl.ds(pl.multiple_of(i * 512 + n * 128, 128), 128)
+                turned = picked[cols, :].T
+                source = source_in[j, pl.ds(i * 4 + n, 1), :]
+                chosen = jnp.where(source == 0, turned[0 : 2 * width], 0.0)
+                for g in range(1, 8):
+                    chosen = jnp.where(source == g, turned[2 * width * g : 2 * width * (g + 1)], chosen)
+                if j:
+                    ready[j, :, cols] = chosen
+                else:
+                    r_ref[x_rows(x), cols] = chosen[by_x]
+                    r_ref[z_rows(z), cols] = chosen[by_z]
             return 0
 
-        lax.fori_loop(0, points // 128, pick, 0)
-
-        def lay(i, _, k=k):
-            cols = pl.ds(pl.multiple_of(i * 128, 128), 128)
-            turned = picked[pl.ds(pl.multiple_of(i * 128, 128), 128), :].T
-            if k:
-                ready[k, :, cols] = turned
-            else:
-                r_ref[mine, cols] = turned
-            return 0
-
-        lax.fori_loop(0, points // 128, lay, 0)
-        if k:
-            copy = pltpu.make_async_remote_copy(
-                src_ref=ready.at[k], dst_ref=r_ref.at[mine, :],
-                send_sem=back_send.at[k], recv_sem=back_recv.at[k],
-                device_id=on_x(k), device_id_type=MESH,
-            )
-            copy.start()
-            back_copies.append(copy)
+        lax.fori_loop(0, points // 512, lay, 0)
+        if j:
+            peer = on_diagonal(j)
+            back_copies.append(remote(ready.at[j, by_x], r_ref.at[x_rows(x), :], back_send.at[0, j], back_recv.at[0, j], peer))
+            back_copies.append(remote(ready.at[j, by_z], r_ref.at[z_rows(z), :], back_send.at[1, j], back_recv.at[1, j], peer))
     for copy in back_copies:
         copy.wait()
 
@@ -342,7 +370,6 @@
     rhs, points = observations.shape
     leaves, leaf = leaf_blocks.shape[:2]
     rank = factors.shape[0] * factors.shape[1]
-    width = rhs // 4
     vector = pltpu.VMEM((rhs, points), F32)
     dma = pltpu.SemaphoreType.DMA
     vmem = pl.BlockSpec(memory_space=pltpu.VMEM)
@@ -360,12 +387,13 @@
             pltpu.VMEM((rank, points), BF16),
             pltpu.VMEM((points, rank), BF16),
             pltpu.VMEM((points, rank), BF16),
-            pltpu.VMEM((16, width, points), F32),
-            pltpu.VMEM((16 * points, width), F32),
-            pltpu.VMEM((points, width), F32),
+            pltpu.VMEM((16, rhs // 4, points), F32),
+            pltpu.VMEM((2 * points, 128), F32),
+            pltpu.VMEM((points, 128), F32),
+            pltpu.VMEM((4, points // 128, 128), jnp.int32),
             pltpu.VMEM((4, points // 128, 128), jnp.int32),
             pltpu.SMEM((4, points // 128, 128), jnp.int32),
-            pltpu.VMEM((4, width, points), F32),
+            pltpu.VMEM((4, rhs // 4, points), F32),
             vector, vector, vector, vector, vector,
             pltpu.VMEM((rhs, rank), F32),
             pltpu.VMEM((2, 4, rhs, rank), F32),
@@ -376,8 +404,8 @@
             pltpu.VMEM((2, 2, rhs, 2 * rhs), F32),
             pltpu.VMEM((2, 4, rhs, rank // 2), F32),
             pltpu.VMEM((2, 4, rhs, 2 * rhs), F32),
-            dma((2,)), dma((4,)), dma((4,)), dma((4,)),
-            dma((16,)), dma((16,)), dma((4,)), dma((4,)),
+            dma((2,)), dma, dma((4,)), dma((4,)),
+            dma((2, 4)), dma((2, 4)), dma((2, 4, 4)), dma((2, 4, 4)), dma((2, 4)), dma((2, 4)),
             dma((8, 4)), dma((8, 2, 4)),
         ],
         compiler_params=pltpu.CompilerParams(

time: 180 us -> 152 us (0.84)
  Pallas kernels: 175 us -> 147 us
    pallas_call x1, Pallas kernels: 175 us -> 147 us  [shards(): pl.pallas_call(kernel, out_shape=(out, out), in_specs=[vmem, vmem, pl.Blo...]
where the time goes in v2:
time: 152 us
  Pallas kernels  147 us (97%)
  local copies, waits for them, and re-layouts  3.74 us (2%)
    pallas_call x1, Pallas kernels, shards(): pl.pallas_call(kernel, out_shape=(out, out), in_specs=[vmem, vmem, pl.Blo...  147 us
    unnamed x2, local copies, waits for them, and re-layouts  3.74 us

profile of v2, /device:TPU:1, one launch (start us, length us, event | category | flops | bytes accessed | tf_op | source)
XLA Modules:
  0.0 151.7 jit_solution(18059057533424872807)
XLA Ops:
  0.6 147.3 %block_cg.1 = (f32[64,2048]{1,0:T(8,128)}, f32[64,2048]{1,0:T(8,128)}) custom-call(f32[64,2048]{1,0:T(8,128)} %obs_ref.1, s32[16,128]{1,0:T(8,128)} %bitcast.3, f32[2,1024,1024]{2,1,0:T(8,128)} %leaf_ref.1, f32[256,2048]{1,0:T(8,128)} %bitcast.2), custom_call_target="tpu_custom_call" | custom-call | tf_op jit(solution)/shard_map/block_cg/pallas_call | solution.py:377
  148.0 1.9 %copy.8 = f32[64,2048]{1,0:T(8,128)} copy(f32[64,2048]{1,0:T(8,128)} %get-tuple-element.4) | data formatting | bytes 1048576
  149.9 1.9 %copy.9 = f32[64,2048]{1,0:T(8,128)} copy(f32[64,2048]{1,0:T(8,128)} %get-tuple-element.5) | data formatting | bytes 1048576

commit v3 on v2

v3 whole, which is shorter than its diff:
```python
import functools

import jax
import jax.numpy as jnp
from jax import lax
from jax.experimental import pallas as pl
from jax.experimental.pallas import tpu as pltpu
from jax.sharding import PartitionSpec as P

ITERS = 4
FAR_FIRST = (10, 2, 8, 6, 14, 9, 11, 3, 7, 13, 15, 12, 5, 1, 4)
MESH = pl.DeviceIdType.MESH
F32 = jnp.float32
BF16 = jnp.bfloat16
EXACT = lax.Precision.HIGHEST
NT = (((1,), (1,)), ((), ()))


def halves(x):
    high = x.astype(BF16)
    return high, (x - high.astype(F32)).astype(BF16)


def dot3(left, right_high, right_low, dims=(((1,), (0,)), ((), ()))):
    rows = left.shape[0]
    high, low = halves(left)
    both = lax.dot_general(
        jnp.concatenate([high, low], 0), right_high, dims, preferred_element_type=F32
    )
    rest = lax.dot_general(high, right_low, dims, preferred_element_type=F32)
    return both[:rows] + (both[rows:] + rest)


def dot_exact(left, right, dims=(((1,), (0,)), ((), ()))):
    return lax.dot_general(left, right, dims, precision=EXACT, preferred_element_type=F32)


def eliminate(systems):
    size, lanes = systems[0].shape
    rows = lax.broadcasted_iota(jnp.int32, (8, lanes), 0)
    tiled = [[system[t : t + 8, :] for t in range(0, size, 8)] for system in systems]
    for k in range(0, size, 4):
        home, first = k // 8, k % 8
        done = []
        for tiles in tiled:
            columns = [
                [jnp.broadcast_to(tile[:, k + j : k + j + 1], (8, lanes)) for tile in tiles] for j in range(4)
            ]
            pivot = [[columns[j][home][first + i : first + i + 1, :] for j in range(4)] for i in range(4)]
            solved = [tiles[home][first + i : first + i + 1, :] for i in range(4)]
            for p in range(4):
                inverse = 1.0 / pivot[p][p]
                solved[p] = solved[p] * inverse
                scaled = [pivot[p][q] * inverse for q in range(p + 1, 4)]
                for i in range(4):
                    if i != p:
                        factor = pivot[i][p]
                        solved[i] = solved[i] - factor * solved[p]
                        for q in range(p + 1, 4):
                            pivot[i][q] = pivot[i][q] - factor * scaled[q - p - 1]
                for q in range(p + 1, 4):
                    pivot[p][q] = scaled[q - p - 1]
            fresh = []
            for t, tile in enumerate(tiles):
                tile = tile - (
                    (columns[0][t] * solved[0] + columns[1][t] * solved[1])
                    + (columns[2][t] * solved[2] + columns[3][t] * solved[3])
                )
                if t == home:
                    for i in range(4):
                        tile = jnp.where(rows == first + i, solved[i], tile)
                fresh.append(tile)
            done.append(fresh)
        tiled = done
    return [jnp.concatenate(tiles, 0) for tiles in tiled]


def total_of(pieces):
    while len(pieces) > 1:
        pieces = [pieces[i] + pieces[i + 1] for i in range(0, len(pieces), 2)]
    return pieces[0]


def fold(both):
    size = both.shape[0]
    row = lax.broadcasted_iota(jnp.int32, both.shape, 0)
    lane = lax.broadcasted_iota(jnp.int32, both.shape, 1)
    second = pltpu.roll(both, size, 1)
    merged = jnp.where(row >= lane, both, second)
    diagonal = jnp.sum(jnp.where(row == lane, second, 0.0), axis=0, keepdims=True)
    top, bottom = merged[: size // 2], pltpu.roll(merged[size // 2 :], size, 1)
    packed = jnp.where(lane[: size // 2] < size, top, bottom)
    return jnp.concatenate([packed, jnp.broadcast_to(diagonal, (8, 2 * size))], 0)


def unfold(packed):
    size = packed.shape[1] // 2
    top = packed[: size // 2]
    merged = jnp.concatenate([top, pltpu.roll(top, size, 1)], 0)[:, :size]
    turned = merged.T
    row = lax.broadcasted_iota(jnp.int32, merged.shape, 0)
    lane = lax.broadcasted_iota(jnp.int32, merged.shape, 1)
    diagonal = jnp.broadcast_to(packed[size // 2 : size // 2 + 1, :size], merged.shape)
    first = jnp.where(row >= lane, merged, turned)
    second = jnp.where(row == lane, diagonal, jnp.where(row < lane, merged, turned))
    return first, second


def kernel(
    obs_ref, order_ref, leaf_ref, factors_ref,
    solution_ref, residual_ref,
    stage, leaf_high, leaf_low, basis_high, basis_low, across_high, across_low,
    gathered, table, picked, order_in, source_in, order_smem, ready,
    r_ref, w_ref, d_ref, s_ref, x_ref, coef_ref, factor_ref,
    c_own, c_in, c_out, c_group, c_all, p_sum, c_sum, y_sum,
    load_sem, smem_sem, order_send, order_recv, near_send, near_recv, far_send, far_recv, back_send, back_recv,
    ring_send, ring_recv, plane_send, plane_recv, coef_send, coef_recv,
):
    group, sub = lax.axis_index("group"), lax.axis_index("sub")
    x = lax.rem(sub, 4)
    z = lax.div(sub, 4)
    core = lax.rem(group, 2)
    y = lax.div(group, 2)
    rhs, points = obs_ref.shape
    rank = factors_ref.shape[0]

    loads = [
        pltpu.make_async_copy(leaf_ref.at[b], stage.at[b], load_sem.at[b]) for b in range(2)
    ]
    for load in loads:
        load.start()

    def on_x(k):
        return (group, z * 4 + (x ^ k))

    def on_z(k):
        return (group, (z ^ k) * 4 + x)

    def on_group(k):
        return (group ^ k, sub)

    def on_plane(k):
        return (group, sub ^ k)

    def on_core(k):
        return (y * 2 + (core ^ k), sub)

    def on_y(k):
        return ((y ^ k) * 2 + core, sub)

    def on_diagonal(j):
        return (group, lax.rem(z + j, 4) * 4 + lax.rem(x + j, 4))

    barrier = pltpu.get_barrier_semaphore()
    for peer in [on_plane(k) for k in range(1, 16)] + [on_group(k) for k in range(1, 8)]:
        pl.semaphore_signal(barrier, inc=1, device_id=peer, device_id_type=MESH)
    pl.semaphore_wait(barrier, 22)

    def remote(source, target, sent, received, peer):
        copy = pltpu.make_async_remote_copy(
            src_ref=source, dst_ref=target, send_sem=sent, recv_sem=received,
            device_id=peer, device_id_type=MESH,
        )
        copy.start()
        return copy

    width = rhs // 8
    by_x, by_z = slice(0, width), slice(width, 2 * width)

    def x_rows(at):
        return pl.ds(pl.multiple_of(at * width, width), width)

    def z_rows(at):
        return pl.ds(pl.multiple_of(rhs // 2 + at * width, width), width)

    order_copies = [
        remote(order_ref, order_in.at[4 - j], order_send.at[j], order_recv.at[4 - j], on_diagonal(j))
        for j in range(1, 4)
    ]
    near = []
    for k in range(1, 4):
        near.append((
            remote(obs_ref.at[x_rows(x ^ k), :], gathered.at[sub, by_x], near_send.at[0, k], near_recv.at[0, k], on_x(k)),
            remote(obs_ref.at[z_rows(z ^ k), :], gathered.at[sub, by_z], near_send.at[1, k], near_recv.at[1, k], on_z(k)),
        ))
    far = []
    for m in range(1, 4):
        far.append(remote(obs_ref.at[x_rows(x), :], gathered.at[sub, by_x], far_send.at[0, 0, m], far_recv.at[0, 0, m], on_z(m)))
        far.append(remote(obs_ref.at[z_rows(z), :], gathered.at[sub, by_z], far_send.at[1, 0, m], far_recv.at[1, 0, m], on_x(m)))
    gathered[sub, by_x, :] = obs_ref[x_rows(x), :]
    gathered[sub, by_z, :] = obs_ref[z_rows(z), :]

    def cut_leaf(b):
        loads[b].wait()

        def cut(i, _):
            rows = pl.ds(pl.multiple_of(i * 64, 64), 64)
            leaf_high[b, rows, :], leaf_low[b, rows, :] = halves(stage[b, rows, :])
            return 0

        lax.fori_loop(0, leaf_ref.shape[1] // 64, cut, 0)

    cut_leaf(0)
    for k in range(1, 4):
        from_x, from_z = near[k - 1]
        from_x.wait()
        slot = gathered.at[z * 4 + (x ^ k), by_x]
        for m in range(1, 4):
            far.append(remote(slot, slot, far_send.at[0, k, m], far_recv.at[0, k, m], on_z(m)))
        from_z.wait()
        slot = gathered.at[(z ^ k) * 4 + x, by_z]
        for m in range(1, 4):
            far.append(remote(slot, slot, far_send.at[1, k, m], far_recv.at[1, k, m], on_x(m)))

    order_in[0] = order_ref[...]
    for copy in order_copies:
        copy.wait()
    for j in range(4):
        position = order_in[j]
        source_in[j] = lax.rem(lax.div(position, points), 8)
        order_in[j] = lax.div(position, points * 8) * points + lax.rem(position, points)
    to_scalar = pltpu.make_async_copy(order_in, order_smem, smem_sem)
    to_scalar.start()
    cut_leaf(1)

    def turn(i, _):
        cols = pl.ds(pl.multiple_of(i * 128, 128), 128)
        part = factors_ref[:, cols]
        basis_high[:, cols], basis_low[:, cols] = halves(part)
        across_high[cols, :], across_low[cols, :] = halves(part.T)
        return 0

    lax.fori_loop(0, points // 128, turn, 0)
    to_scalar.wait()
    for copy in far:
        copy.wait()

    def tabulate(i, _):
        for j in range(4):
            cols = pl.ds(pl.multiple_of(i * 512 + j * 128, 128), 128)
            for h in range(2):
                rows = pl.ds(pl.multiple_of(h * points + i * 512 + j * 128, 128), 128)
                table[rows, :] = gathered[8 * h : 8 * h + 8, :, cols].reshape(128, 128).T
        return 0

    lax.fori_loop(0, points // 512, tabulate, 0)

    back_copies = []
    for j in (2, 1, 3, 0):

        def pick(i, _, j=j):
            for n in range(128):
                picked[pl.ds(i * 128 + n, 1), :] = table[pl.ds(order_smem[j, i, n], 1), :]
            return 0

        lax.fori_loop(0, points // 128, pick, 0)

        def lay(i, _, j=j):
            for n in range(4):
                cols = pl.ds(pl.multiple_of(i * 512 + n * 128, 128), 128)
                turned = picked[cols, :].T
                source = source_in[j, pl.ds(i * 4 + n, 1), :]
                chosen = jnp.where(source == 0, turned[0 : 2 * width], 0.0)
                for g in range(1, 8):
                    chosen = jnp.where(source == g, turned[2 * width * g : 2 * width * (g + 1)], chosen)
                if j:
                    ready[j, :, cols] = chosen
                else:
                    r_ref[0, x_rows(x), cols] = chosen[by_x]
                    r_ref[0, z_rows(z), cols] = chosen[by_z]
            return 0

        lax.fori_loop(0, points // 512, lay, 0)
        if j:
            peer = on_diagonal(j)
            back_copies.append(remote(ready.at[j, by_x], r_ref.at[0, x_rows(x), :], back_send.at[0, j], back_recv.at[0, j], peer))
            back_copies.append(remote(ready.at[j, by_z], r_ref.at[0, z_rows(z), :], back_send.at[1, j], back_recv.at[1, j], peer))
    for copy in back_copies:
        copy.wait()

    def send(kind, turn_at, buffer, slot, peer, count):
        copies = []
        for k in range(1, count):
            copy = pltpu.make_async_remote_copy(
                src_ref=buffer.at[turn_at, slot], dst_ref=buffer.at[turn_at, slot],
                send_sem=ring_send.at[kind, k], recv_sem=ring_recv.at[kind, turn_at, k],
                device_id=peer(k), device_id_type=MESH,
            )
            copy.start()
            copies.append(copy)
        return copies

    def finish(copies):
        for copy in copies:
            copy.wait()

    d_ref[...] = jnp.zeros_like(d_ref)
    s_ref[...] = jnp.zeros_like(s_ref)
    x_ref[...] = jnp.zeros_like(x_ref)
    half = points // 2
    eye = (lax.broadcasted_iota(jnp.int32, (rhs, rhs), 0) == lax.broadcasted_iota(jnp.int32, (rhs, rhs), 1)).astype(F32)

    piece_lane = lax.broadcasted_iota(jnp.int32, (8, 128), 1)

    def by_level(parts):
        return jnp.where(
            piece_lane < 64,
            jnp.where(piece_lane < 32, parts[0], parts[1]),
            jnp.where(piece_lane < 96, parts[2], parts[3]),
        )

    def coef_scatter(at, own):
        for j in range(16):
            c_own[at, j] = own[8 * (j % 8) : 8 * (j % 8) + 8, 128 * (j // 8) : 128 * (j // 8) + 128]
        copies = [
            remote(c_own.at[at, sub ^ k], c_in.at[at, sub], coef_send.at[0, k], coef_recv.at[at, 0, k], on_plane(k))
            for k in FAR_FIRST
        ]
        c_in[at, sub] = c_own[at, sub]
        return copies

    def coef_groups(at, copies):
        finish(copies)
        sums = [[c_in[at, m] for m in range(16)]]
        for _ in range(4):
            sums.append([sums[-1][i] + sums[-1][i + 1] for i in range(0, len(sums[-1]), 2)])
        for m in range(16):
            c_out[at, m] = by_level([sums[level][m >> level] for level in range(4)])
        c_group[at, group] = sums[4][0]
        return [
            remote(c_group.at[at, group], c_group.at[at, group], coef_send.at[1, k], coef_recv.at[at, 1, k], on_group(k))
            for k in (6, 7, 4, 5, 2, 3, 1)
        ]

    def coef_return(at, copies):
        finish(copies)
        own = [c_group[at, group ^ k] for k in range(8)]
        pair = own[0] + own[1]
        four = pair + (own[2] + own[3])
        upper = by_level([own[0], pair, four, four + ((own[4] + own[5]) + (own[6] + own[7]))])
        for m in range(16):
            c_out[at, m] = jnp.where(sub < 8, c_out[at, m], upper)
        copies = [
            remote(c_out.at[at, sub ^ k], c_all.at[at, sub], coef_send.at[2, k], coef_recv.at[at, 2, k], on_plane(k))
            for k in FAR_FIRST
        ]
        c_all[at, sub] = c_out[at, sub]
        return copies

    def coef_whole(at, copies):
        finish(copies)
        return jnp.concatenate(
            [jnp.concatenate([c_all[at, j], c_all[at, j + 8]], 1) for j in range(8)], 0
        )

    def leaf_product(now):
        for b in range(2):
            cols = slice(b * half, (b + 1) * half)
            w_ref[:, cols] = dot3(r_ref[now, :, cols], leaf_high[b], leaf_low[b])

    def weights(matrix):
        high, low = halves(matrix)
        high, low = high.astype(F32), low.astype(F32)
        return jnp.concatenate([high, high, low, low], 0).T.astype(BF16)

    def times(weight, array):
        high, low = halves(array)
        return jnp.dot(
            weight, jnp.concatenate([high, low, high, low], 0), preferred_element_type=F32
        )

    def by_columns(step):
        def body(c, _):
            step(pl.ds(pl.multiple_of(c * 512, 512), 512))
            return 0

        lax.fori_loop(0, points // 512, body, 0)

    def advance_solution(before):
        def step(cols):
            fresh = r_ref[before, :, cols] + times(factor_ref[0], d_ref[:, cols])
            d_ref[:, cols] = fresh
            x_ref[:, cols] = x_ref[:, cols] + times(factor_ref[1], fresh)

        by_columns(step)

    copies = coef_scatter(1, dot3(r_ref[0], across_high[...], across_low[...]))
    leaf_product(0)
    coef_ref[0] = coef_whole(1, coef_return(1, coef_groups(1, copies)))
    coef_ref[1] = jnp.zeros((rhs, rank), F32)
    factor_ref[...] = jnp.zeros_like(factor_ref)

    def iteration(step, carry, more):
        inverse, curv_before = carry
        at = lax.rem(step, 2)
        now, later = at, 1 - at

        for c in range(4):
            cols = slice(c * 512, (c + 1) * 512)
            w_ref[:, cols] = w_ref[:, cols] + dot3(coef_ref[0], basis_high[:, cols], basis_low[:, cols])
        if more:
            copies = coef_scatter(at, dot3(w_ref[...], across_high[...], across_low[...]))

        rw_high, rw_low = halves(jnp.concatenate([r_ref[now], w_ref[...]], 0))
        p_sum[at, sub] = fold(dot3(r_ref[now], rw_high, rw_low, NT))
        sums = [
            remote(p_sum.at[at, sub], p_sum.at[at, sub], plane_send.at[k], plane_recv.at[at, k], on_plane(k))
            for k in FAR_FIRST
        ]
        if more:
            copies = coef_groups(at, copies)

        finish(sums)
        c_sum[at, core] = total_of([p_sum[at, m] for m in range(16)])
        sums = send(5, at, c_sum, core, on_core, 2)
        finish(sums)
        y_sum[at, y] = c_sum[at, 0] + c_sum[at, 1]
        sums = send(7, at, y_sum, y, on_y, 4)

        @pl.when(step > 0)
        def _():
            advance_solution(later)

        if more:
            copies = coef_return(at, copies)
        finish(sums)
        norm, along = unfold(total_of([y_sum[at, m] for m in range(4)]))
        beta = dot_exact(inverse, norm)
        beta_weight = weights(beta)
        factor_ref[0] = beta_weight
        curv = along - dot_exact(beta.T, dot_exact(curv_before, beta))

        def advance(cols):
            s_ref[:, cols] = w_ref[:, cols] + times(beta_weight, s_ref[:, cols])

        by_columns(advance)
        systems = [jnp.concatenate([curv, norm], 1)]
        if more:
            systems.append(jnp.concatenate([norm, eye], 1))
        done = eliminate(systems)
        alpha = done[0][:, rhs:]
        alpha_weight = weights(alpha)
        factor_ref[1] = alpha_weight

        def improve(cols):
            r_ref[later, :, cols] = r_ref[now, :, cols] - times(alpha_weight, s_ref[:, cols])

        by_columns(improve)
        if more:
            coef_ref[1] = coef_whole(at, copies) + dot_exact(beta.T, coef_ref[1])
            coef_ref[0] = coef_ref[0] - dot_exact(alpha.T, coef_ref[1])
            leaf_product(later)
        return done[-1][:, rhs:], curv

    zeros = jnp.zeros((rhs, rhs), F32)
    carry = lax.fori_loop(0, ITERS - 1, functools.partial(iteration, more=True), (zeros, zeros))
    iteration(ITERS - 1, carry, False)
    advance_solution((ITERS - 1) % 2)
    solution_ref[...] = x_ref[...]
    residual_ref[...] = r_ref[ITERS % 2]


def shards(observations, order, leaf_blocks, factors):
    rhs, points = observations.shape
    leaves, leaf = leaf_blocks.shape[:2]
    rank = factors.shape[0] * factors.shape[1]
    vector = pltpu.VMEM((rhs, points), F32)
    dma = pltpu.SemaphoreType.DMA
    vmem = pl.BlockSpec(memory_space=pltpu.VMEM)
    out = jax.ShapeDtypeStruct((rhs, points), F32)
    return pl.pallas_call(
        kernel,
        out_shape=(out, out),
        in_specs=[vmem, vmem, pl.BlockSpec(memory_space=pl.ANY), vmem],
        out_specs=(vmem, vmem),
        scratch_shapes=[
            pltpu.VMEM((leaves, leaf, leaf), F32),
            pltpu.VMEM((leaves, leaf, leaf), BF16),
            pltpu.VMEM((leaves, leaf, leaf), BF16),
            pltpu.VMEM((rank, points), BF16),
            pltpu.VMEM((rank, points), BF16),
            pltpu.VMEM((points, rank), BF16),
            pltpu.VMEM((points, rank), BF16),
            pltpu.VMEM((16, rhs // 4, points), F32),
            pltpu.VMEM((2 * points, 128), F32),
            pltpu.VMEM((points, 128), F32),
            pltpu.VMEM((4, points // 128, 128), jnp.int32),
            pltpu.VMEM((4, points // 128, 128), jnp.int32),
            pltpu.SMEM((4, points // 128, 128), jnp.int32),
            pltpu.VMEM((4, rhs // 4, points), F32),
            pltpu.VMEM((2, rhs, points), F32), vector, vector, vector, vector,
            pltpu.VMEM((2, rhs, rank), F32),
            pltpu.VMEM((2, rhs, 4 * rhs), BF16),
            pltpu.VMEM((2, 16, 8, 128), F32),
            pltpu.VMEM((2, 16, 8, 128), F32),
            pltpu.VMEM((2, 16, 8, 128), F32),
            pltpu.VMEM((2, 8, 8, 128), F32),
            pltpu.VMEM((2, 16, 8, 128), F32),
            pltpu.VMEM((2, 16, rhs // 2 + 8, 2 * rhs), F32),
            pltpu.VMEM((2, 2, rhs // 2 + 8, 2 * rhs), F32),
            pltpu.VMEM((2, 4, rhs // 2 + 8, 2 * rhs), F32),
            dma((2,)), dma, dma((4,)), dma((4,)),
            dma((2, 4)), dma((2, 4)), dma((2, 4, 4)), dma((2, 4, 4)), dma((2, 4)), dma((2, 4)),
            dma((8, 4)), dma((8, 2, 4)), dma((16,)), dma((2, 16)),
            dma((3, 16)), dma((2, 3, 16)),
        ],
        compiler_params=pltpu.CompilerParams(
            collective_id=0, has_side_effects=True, vmem_limit_bytes=60 * 2**20
        ),
        name="block_cg",
    )(observations, order.reshape(points // 128, 128), leaf_blocks, factors.reshape(rank, points))


def solution(mesh):
    in_specs = (
        P(None, ("group", "sub")),
        P(("group", "sub")),
        P(("group", "sub"), None, None),
        P(None, None, ("group", "sub")),
    )
    out_specs = (P(None, ("group", "sub")), P(None, ("group", "sub")))
    return jax.shard_map(shards, mesh=mesh, in_specs=in_specs, out_specs=out_specs, check_vma=False)
```

time: 152 us -> 139 us (0.914)
  Pallas kernels: 147 us -> 135 us
    pallas_call x1, Pallas kernels: 147 us -> 135 us  [shards(): pl.pallas_call(kernel, out_shape=(out, out), in_specs=[vmem, vmem, pl.Blo...]
where the time goes in v3:
time: 139 us
  Pallas kernels  135 us (97%)
  local copies, waits for them, and re-layouts  3.74 us (3%)
    pallas_call x1, Pallas kernels, shards(): pl.pallas_call(kernel, out_shape=(out, out), in_specs=[vmem, vmem, pl.Blo...  135 us
    unnamed x2, local copies, waits for them, and re-layouts  3.74 us

profile of v3, /device:TPU:1, one launch (start us, length us, event | category | flops | bytes accessed | tf_op | source)
XLA Modules:
  0.0 139.2 jit_solution(8846583594905094914)
XLA Ops:
  0.6 134.8 %block_cg.1 = (f32[64,2048]{1,0:T(8,128)}, f32[64,2048]{1,0:T(8,128)}) custom-call(f32[64,2048]{1,0:T(8,128)} %obs_ref.1, s32[16,128]{1,0:T(8,128)} %bitcast.3, f32[2,1024,1024]{2,1,0:T(8,128)} %leaf_ref.1, f32[256,2048]{1,0:T(8,128)} %bitcast.2), custom_call_target="tpu_custom_call" | custom-call | tf_op jit(solution)/shard_map/block_cg/pallas_call | solution.py:471
  135.5 1.9 %copy.8 = f32[64,2048]{1,0:T(8,128)} copy(f32[64,2048]{1,0:T(8,128)} %get-tuple-element.4) | data formatting | bytes 1048576
  137.4 1.9 %copy.9 = f32[64,2048]{1,0:T(8,128)} copy(f32[64,2048]{1,0:T(8,128)} %get-tuple-element.5) | data formatting | bytes 1048576

commit v4 on v3

--- a/solution.py
+++ b/solution.py
@@ -398,9 +398,6 @@
         for c in range(4):
             cols = slice(c * 512, (c + 1) * 512)
             w_ref[:, cols] = w_ref[:, cols] + dot3(coef_ref[0], basis_high[:, cols], basis_low[:, cols])
-        if more:
-            copies = coef_scatter(at, dot3(w_ref[...], across_high[...], across_low[...]))
-
         rw_high, rw_low = halves(jnp.concatenate([r_ref[now], w_ref[...]], 0))
         p_sum[at, sub] = fold(dot3(r_ref[now], rw_high, rw_low, NT))
         sums = [
@@ -408,11 +405,14 @@
             for k in FAR_FIRST
         ]
         if more:
-            copies = coef_groups(at, copies)
+            copies = coef_scatter(at, dot3(w_ref[...], across_high[...], across_low[...]))
 
         finish(sums)
         c_sum[at, core] = total_of([p_sum[at, m] for m in range(16)])
         sums = send(5, at, c_sum, core, on_core, 2)
+        if more:
+            copies = coef_groups(at, copies)
+
         finish(sums)
         y_sum[at, y] = c_sum[at, 0] + c_sum[at, 1]
         sums = send(7, at, y_sum, y, on_y, 4)

time: 139 us -> 138 us (level)
  Pallas kernels: 135 us -> 133 us
    pallas_call x1, Pallas kernels: 135 us -> 133 us  [shards(): pl.pallas_call(kernel, out_shape=(out, out), in_specs=[vmem, vmem, pl.Blo...]
where the time goes in v4:
time: 138 us; the launch traced here: 137 us
  Pallas kernels  133 us (96%)
  local copies, waits for them, and re-layouts  3.74 us (3%)
    pallas_call x1, Pallas kernels, shards(): pl.pallas_call(kernel, out_shape=(out, out), in_specs=[vmem, vmem, pl.Blo...  133 us
    unnamed x2, local copies, waits for them, and re-layouts  3.74 us

profile of v4, /device:TPU:1, one launch (start us, length us, event | category | flops | bytes accessed | tf_op | source)
XLA Modules:
  0.0 137.4 jit_solution(17080832347222472306)
XLA Ops:
  0.6 133.0 %block_cg.1 = (f32[64,2048]{1,0:T(8,128)}, f32[64,2048]{1,0:T(8,128)}) custom-call(f32[64,2048]{1,0:T(8,128)} %obs_ref.1, s32[16,128]{1,0:T(8,128)} %bitcast.3, f32[2,1024,1024]{2,1,0:T(8,128)} %leaf_ref.1, f32[256,2048]{1,0:T(8,128)} %bitcast.2), custom_call_target="tpu_custom_call" | custom-call | tf_op jit(solution)/shard_map/block_cg/pallas_call | solution.py:471
  133.6 1.9 %copy.8 = f32[64,2048]{1,0:T(8,128)} copy(f32[64,2048]{1,0:T(8,128)} %get-tuple-element.4) | data formatting | bytes 1048576
  135.5 1.9 %copy.9 = f32[64,2048]{1,0:T(8,128)} copy(f32[64,2048]{1,0:T(8,128)} %get-tuple-element.5) | data formatting | bytes 1048576

commit v5 on v4

--- a/solution.py
+++ b/solution.py
@@ -107,9 +107,9 @@
 
 
 def kernel(
-    obs_ref, order_ref, leaf_ref, factors_ref,
+    obs_far, order_far, leaf_ref, factors_far,
     solution_ref, residual_ref,
-    stage, leaf_high, leaf_low, basis_high, basis_low, across_high, across_low,
+    obs_ref, order_ref, factors_ref, stage, leaf_high, leaf_low, basis_high, basis_low, across_high, across_low,
     gathered, table, picked, order_in, source_in, order_smem, ready,
     r_ref, w_ref, d_ref, s_ref, x_ref, coef_ref, factor_ref,
     c_own, c_in, c_out, c_group, c_all, p_sum, c_sum, y_sum,
@@ -124,10 +124,13 @@
     rhs, points = obs_ref.shape
     rank = factors_ref.shape[0]
 
+    obs_load = pltpu.make_async_copy(obs_far, obs_ref, load_sem.at[2])
+    order_load = pltpu.make_async_copy(order_far, order_ref, load_sem.at[3])
+    factors_load = pltpu.make_async_copy(factors_far, factors_ref, load_sem.at[4])
     loads = [
         pltpu.make_async_copy(leaf_ref.at[b], stage.at[b], load_sem.at[b]) for b in range(2)
     ]
-    for load in loads:
+    for load in [order_load, obs_load, *loads, factors_load]:
         load.start()
 
     def on_x(k):
@@ -154,6 +157,8 @@
     barrier = pltpu.get_barrier_semaphore()
     for peer in [on_plane(k) for k in range(1, 16)] + [on_group(k) for k in range(1, 8)]:
         pl.semaphore_signal(barrier, inc=1, device_id=peer, device_id_type=MESH)
+    order_load.wait()
+    obs_load.wait()
     pl.semaphore_wait(barrier, 22)
 
     def remote(source, target, sent, received, peer):
@@ -230,6 +235,7 @@
         across_high[cols, :], across_low[cols, :] = halves(part.T)
         return 0
 
+    factors_load.wait()
     lax.fori_loop(0, points // 128, turn, 0)
     to_scalar.wait()
     for copy in far:
@@ -455,9 +461,13 @@
     zeros = jnp.zeros((rhs, rhs), F32)
     carry = lax.fori_loop(0, ITERS - 1, functools.partial(iteration, more=True), (zeros, zeros))
     iteration(ITERS - 1, carry, False)
+    residual_out = pltpu.make_async_copy(r_ref.at[ITERS % 2], residual_ref, load_sem.at[0])
+    residual_out.start()
     advance_solution((ITERS - 1) % 2)
-    solution_ref[...] = x_ref[...]
-    residual_ref[...] = r_ref[ITERS % 2]
+    solution_out = pltpu.make_async_copy(x_ref, solution_ref, load_sem.at[1])
+    solution_out.start()
+    residual_out.wait()
+    solution_out.wait()
 
 
 def shards(observations, order, leaf_blocks, factors):
@@ -466,14 +476,17 @@
     rank = factors.shape[0] * factors.shape[1]
     vector = pltpu.VMEM((rhs, points), F32)
     dma = pltpu.SemaphoreType.DMA
-    vmem = pl.BlockSpec(memory_space=pltpu.VMEM)
+    anywhere = pl.BlockSpec(memory_space=pl.ANY)
     out = jax.ShapeDtypeStruct((rhs, points), F32)
     return pl.pallas_call(
         kernel,
         out_shape=(out, out),
-        in_specs=[vmem, vmem, pl.BlockSpec(memory_space=pl.ANY), vmem],
-        out_specs=(vmem, vmem),
+        in_specs=[anywhere] * 4,
+        out_specs=(anywhere, anywhere),
         scratch_shapes=[
+            vector,
+            pltpu.VMEM((points // 128, 128), jnp.int32),
+            pltpu.VMEM((rank, points), F32),
             pltpu.VMEM((leaves, leaf, leaf), F32),
             pltpu.VMEM((leaves, leaf, leaf), BF16),
             pltpu.VMEM((leaves, leaf, leaf), BF16),
@@ -499,7 +512,7 @@
             pltpu.VMEM((2, 16, rhs // 2 + 8, 2 * rhs), F32),
             pltpu.VMEM((2, 2, rhs // 2 + 8, 2 * rhs), F32),
             pltpu.VMEM((2, 4, rhs // 2 + 8, 2 * rhs), F32),
-            dma((2,)), dma, dma((4,)), dma((4,)),
+            dma((5,)), dma, dma((4,)), dma((4,)),
             dma((2, 4)), dma((2, 4)), dma((2, 4, 4)), dma((2, 4, 4)), dma((2, 4)), dma((2, 4)),
             dma((8, 4)), dma((8, 2, 4)), dma((16,)), dma((2, 16)),
             dma((3, 16)), dma((2, 3, 16)),

time: 138 us -> 136 us (0.986)
  Pallas kernels: 133 us -> 131 us
    pallas_call x1, Pallas kernels: 133 us -> 131 us  [shards(): pl.pallas_call(kernel, out_shape=(out, out), in_specs=[anywhere] * 4, out...]
where the time goes in v5:
time: 136 us; the launch traced here: 135 us
  Pallas kernels  131 us (96%)
  local copies, waits for them, and re-layouts  3.74 us (3%)
    pallas_call x1, Pallas kernels, shards(): pl.pallas_call(kernel, out_shape=(out, out), in_specs=[anywhere] * 4, out...  131 us
    unnamed x2, local copies, waits for them, and re-layouts  3.74 us

profile of v5, /device:TPU:1, one launch (start us, length us, event | category | flops | bytes accessed | tf_op | source)
XLA Modules:
  0.0 135.5 jit_solution(3644351562094250338)
XLA Ops:
  0.6 131.1 %block_cg.1 = (f32[64,2048]{1,0:T(8,128)}, f32[64,2048]{1,0:T(8,128)}) custom-call(f32[64,2048]{1,0:T(8,128)} %obs_far.1, s32[16,128]{1,0:T(8,128)} %bitcast.3, f32[2,1024,1024]{2,1,0:T(8,128)} %leaf_ref.1, f32[256,2048]{1,0:T(8,128)} %bitcast.2), custom_call_target="tpu_custom_call" | custom-call | tf_op jit(solution)/shard_map/block_cg/pallas_call | solution.py:481
  131.7 1.9 %copy.8 = f32[64,2048]{1,0:T(8,128)} copy(f32[64,2048]{1,0:T(8,128)} %get-tuple-element.4) | data formatting | bytes 1048576
  133.6 1.9 %copy.9 = f32[64,2048]{1,0:T(8,128)} copy(f32[64,2048]{1,0:T(8,128)} %get-tuple-element.5) | data formatting | bytes 1048576

commit v6 on v5

--- a/solution.py
+++ b/solution.py
@@ -377,10 +377,10 @@
 
     def by_columns(step):
         def body(c, _):
-            step(pl.ds(pl.multiple_of(c * 512, 512), 512))
+            step(pl.ds(pl.multiple_of(c * 1024, 1024), 1024))
             return 0
 
-        lax.fori_loop(0, points // 512, body, 0)
+        lax.fori_loop(0, points // 1024, body, 0)
 
     def advance_solution(before):
         def step(cols):
@@ -429,12 +429,13 @@
 
         if more:
             copies = coef_return(at, copies)
+        curv_inverse = dot_exact(curv_before, inverse)
         finish(sums)
         norm, along = unfold(total_of([y_sum[at, m] for m in range(4)]))
         beta = dot_exact(inverse, norm)
         beta_weight = weights(beta)
         factor_ref[0] = beta_weight
-        curv = along - dot_exact(beta.T, dot_exact(curv_before, beta))
+        curv = along - dot_exact(beta.T, dot_exact(curv_inverse, norm))
 
         def advance(cols):
             s_ref[:, cols] = w_ref[:, cols] + times(beta_weight, s_ref[:, cols])

time: 136 us -> 133 us (0.978)
  Pallas kernels: 131 us -> 128 us
    pallas_call x1, Pallas kernels: 131 us -> 128 us  [shards(): pl.pallas_call(kernel, out_shape=(out, out), in_specs=[anywhere] * 4, out...]
where the time goes in v6:
time: 133 us
  Pallas kernels  128 us (96%)
  local copies, waits for them, and re-layouts  3.74 us (3%)
    pallas_call x1, Pallas kernels, shards(): pl.pallas_call(kernel, out_shape=(out, out), in_specs=[anywhere] * 4, out...  128 us
    unnamed x2, local copies, waits for them, and re-layouts  3.74 us

profile of v6, /device:TPU:1, one launch (start us, length us, event | category | flops | bytes accessed | tf_op | source)
XLA Modules:
  0.0 132.6 jit_solution(10283966487974988780)
XLA Ops:
  0.6 128.3 %block_cg.1 = (f32[64,2048]{1,0:T(8,128)}, f32[64,2048]{1,0:T(8,128)}) custom-call(f32[64,2048]{1,0:T(8,128)} %obs_far.1, s32[16,128]{1,0:T(8,128)} %bitcast.3, f32[2,1024,1024]{2,1,0:T(8,128)} %leaf_ref.1, f32[256,2048]{1,0:T(8,128)} %bitcast.2), custom_call_target="tpu_custom_call" | custom-call | tf_op jit(solution)/shard_map/block_cg/pallas_call | solution.py:482
  128.9 1.9 %copy.8 = f32[64,2048]{1,0:T(8,128)} copy(f32[64,2048]{1,0:T(8,128)} %get-tuple-element.4) | data formatting | bytes 1048576
  130.8 1.9 %copy.9 = f32[64,2048]{1,0:T(8,128)} copy(f32[64,2048]{1,0:T(8,128)} %get-tuple-element.5) | data formatting | bytes 1048576
